TPU v7x, 32 devices: a whole 2x2x4 slice. The times are simulated.
32 devices in a mesh: groups: 2 (over x), ty: 4 (over y, core), tx: 4 (over z).
Axes of the slice: x: 2, y: 2, z: 4, core: 2. Of those that a mesh axis runs over, the one named last changes fastest.
Arguments:
- object_planes: float32 [4, 2048, 1024], P(None, ('groups', 'ty'), 'tx'), parts along dimension 1, may hold values from -5 to 5
- probe: float32 [2, 256, 256], replicated, may hold values from -5 to 5
- phase: float32 [256, 256], replicated, may hold values from -3.140625 to 3.140625
- coords: int32 [8, 4, 4, 2], P(('groups', 'ty'), 'tx'), parts along dimension 0, may hold values from 0 to 255
- live: int32 [8, 4], P(('groups', 'ty'), 'tx'), parts along dimension 0, may hold values from 0 to 4, as said below
- amplitude: float32 [8, 4, 4, 256, 256], P(('groups', 'ty'), 'tx'), parts along dimension 0, may hold values from 0 to 2
Outputs:
- updated: float32 [4, 2048, 1024], P(None, ('groups', 'ty'), 'tx'), parts along dimension 1
There are 2 independent parts, one for each index of `groups`. A program takes and returns all parts, laid end to end along the dimension named above; an argument that names none is the same for every part. Nothing has to cross between parts.
Inputs may be any that keep to these rules, and one draw needn't show every extreme that they name: Only slots below live of their tile are used; some tile holds 4 live slots.
All inputs are finite; a program needn't handle non-finite values.
Results may differ from a plain program's by a relative error of at most 0.0003.
Values sent between devices are 32-bit elements; how exact they have to be, the bound alone decides.
No kernel may reach another device: no remote copies, remote signals or barrier semaphores. Data moves between devices by JAX's collectives and lax.ppermute only.
A program may use at most 128 MiB of HBM per device.

v0:
```python
import functools
import math

import jax
import jax.numpy as jnp
import ml_dtypes
import numpy as np
from jax import lax
from jax.experimental import pallas as pl
from jax.experimental.pallas import tpu as pltpu
from jax.sharding import PartitionSpec as P

F32 = jnp.float32
BF16 = jnp.bfloat16
VMEM = pl.BlockSpec(memory_space=pltpu.VMEM)
SMEM = pl.BlockSpec(memory_space=pltpu.SMEM)


def from_behind(block, axis, distance):
    devices = range(lax.axis_size(axis))
    route = [(i - distance, i) for i in devices if i - distance in devices]
    return lax.ppermute(block, axis, route)


def from_diagonal(block, distance):
    rows, cols = lax.axis_size("ty"), lax.axis_size("tx")
    route = [
        ((i - distance) * cols + j - distance, i * cols + j)
        for i in range(rows)
        for j in range(cols)
        if 0 <= i - distance < rows and 0 <= j - distance < cols
    ]
    return lax.ppermute(block, ("ty", "tx"), route)


def transform_tables(width):
    half = width // 2
    n = np.arange(half)[:, None]
    k = np.arange(half)[None, :]
    out = []
    for odd in (0, 1):
        angle = -2.0 * math.pi * ((n * (2 * k + odd)) % width) / width
        wr, wi = np.cos(angle) / math.sqrt(width), np.sin(angle) / math.sqrt(width)
        real = np.block([[wr, wi], [-wi, wr]])
        head = real.astype(ml_dtypes.bfloat16)
        tail = (real - head.astype(np.float64)).astype(ml_dtypes.bfloat16)
        out += [head, tail]
    out += [np.ascontiguousarray(m.T) for m in out]
    return np.stack(out)


def order_table(width):
    half = width // 2
    table = np.zeros((2, width, width), np.float32)
    source = np.concatenate([np.arange(0, width, 2), np.arange(1, width, 2)])
    table[0, np.arange(width), source] = 1.0
    table[1] = table[0].T
    return table


def split(x):
    head = x.astype(BF16)
    return head, (x - head.astype(F32)).astype(BF16)


def mm(a, b):
    return jnp.dot(a, b, preferred_element_type=F32)


def right_mul(x, table, at):
    head, tail = split(x)
    return mm(head, table[at]) + mm(tail, table[at]) + mm(head, table[at + 1])


def left_mul(x, table, at):
    head, tail = split(x)
    return mm(table[at], head) + mm(table[at], tail) + mm(table[at + 1], head)


def forward(xr, xi, table):
    half = xr.shape[0] // 2
    sr = jnp.concatenate([xr[:half] + xr[half:], xi[:half] + xi[half:]])
    dr = jnp.concatenate([xr[:half] - xr[half:], xi[:half] - xi[half:]])
    even = left_mul(sr, table, 4)
    odd = left_mul(dr, table, 6)
    yr = jnp.concatenate([even[:half], odd[:half]])
    yi = jnp.concatenate([even[half:], odd[half:]])
    sr = jnp.concatenate([yr[:, :half] + yr[:, half:], yi[:, :half] + yi[:, half:]], axis=1)
    dr = jnp.concatenate([yr[:, :half] - yr[:, half:], yi[:, :half] - yi[:, half:]], axis=1)
    even = right_mul(sr, table, 0)
    odd = right_mul(dr, table, 2)
    return (
        jnp.concatenate([even[:, :half], odd[:, :half]], axis=1),
        jnp.concatenate([even[:, half:], odd[:, half:]], axis=1),
    )


def backward(xr, xi, table):
    half = xr.shape[0] // 2
    even = left_mul(jnp.concatenate([xr[:half], xi[:half]]), table, 0)
    odd = left_mul(jnp.concatenate([xr[half:], xi[half:]]), table, 2)
    yr = jnp.concatenate([even[:half] + odd[:half], even[:half] - odd[:half]])
    yi = jnp.concatenate([even[half:] + odd[half:], even[half:] - odd[half:]])
    even = right_mul(jnp.concatenate([yr[:, :half], yi[:, :half]], axis=1), table, 4)
    odd = right_mul(jnp.concatenate([yr[:, half:], yi[:, half:]], axis=1), table, 6)
    return (
        jnp.concatenate([even[:, :half] + odd[:, :half], even[:, :half] - odd[:, :half]], axis=1),
        jnp.concatenate([even[:, half:] + odd[:, half:], even[:, half:] - odd[:, half:]], axis=1),
    )


def wraps(shape, top, left):
    rows = lax.broadcasted_iota(jnp.int32, shape, 0)
    cols = lax.broadcasted_iota(jnp.int32, shape, 1)
    return rows < top, cols < left


def pick(quads, plane, low, right):
    own, east, south, corner = (q[plane] for q in quads)
    return jnp.where(low, jnp.where(right, corner, south), jnp.where(right, east, own))


def deposit(quads, plane, value, low, right):
    own, east, south, corner = quads
    zero = jnp.zeros_like(value)
    upper = jnp.where(low, zero, value)
    lower = jnp.where(low, value, zero)
    own[plane] += jnp.where(right, zero, upper)
    east[plane] += jnp.where(right, upper, zero)
    south[plane] += jnp.where(right, zero, lower)
    corner[plane] += jnp.where(right, lower, zero)


def clear(refs):
    for ref in refs:
        ref[...] = jnp.zeros_like(ref)


def prep_kernel(info, probe, amp, phasor, order, shifted, amp_out, phasor_out):
    slots = amp.shape[0]

    def reorder(x):
        once = jnp.dot(x, order[1], precision=lax.Precision.HIGHEST, preferred_element_type=F32)
        return jnp.dot(order[0], once, precision=lax.Precision.HIGHEST, preferred_element_type=F32)

    for part in range(2):
        phasor_out[part] = reorder(phasor[part])

    def body(s, carry):
        top, left = info[0, 2 * s], info[0, 2 * s + 1]
        for part in range(2):
            shifted[s, part] = pltpu.roll(pltpu.roll(probe[part], top, 0), left, 1)
        amp_out[s] = reorder(amp[s])
        return carry

    lax.fori_loop(0, info[0, 2 * slots], body, 0)


def cover_kernel(info, probe, cover):
    slots = (info.shape[1] - 1) // 2
    cover[...] = jnp.zeros_like(cover)
    for tile in range(4):

        def body(s, carry, tile=tile):
            top, left = info[tile, 2 * s], info[tile, 2 * s + 1]
            power = probe[0] * probe[0] + probe[1] * probe[1]
            moved = pltpu.roll(pltpu.roll(power, top, 0), left, 1)
            low, right = wraps(power.shape, top, left)
            keep = (low if tile >= 2 else ~low) & (right if tile % 2 else ~right)
            cover[...] += jnp.where(keep, moved, 0.0)
            return carry

        lax.fori_loop(0, info[tile, 2 * slots], body, 0)


def first_kernel(info, own, east, south, corner, shifted, phasor, table, wave, p_own, p_east, p_south, p_corner):
    slots = shifted.shape[0]
    quads_in = (own, east, south, corner)
    quads = (p_own, p_east, p_south, p_corner)
    clear(quads)

    def body(s, carry):
        low, right = wraps(own.shape[1:], info[0, 2 * s], info[0, 2 * s + 1])
        fr, fi = pick(quads_in, 0, low, right), pick(quads_in, 1, low, right)
        pr, pi = shifted[s, 0], shifted[s, 1]
        ur, ui = forward(pr * fr - pi * fi, pr * fi + pi * fr, table)
        hr, hi = phasor[0], phasor[1]
        wr, wi = backward(ur * hr - ui * hi, ur * hi + ui * hr, table)
        wave[s, 0] = wr
        wave[s, 1] = wi
        deposit(quads, 0, wr * wr + wi * wi, low, right)
        return carry

    lax.fori_loop(0, info[0, 2 * slots], body, 0)


def second_kernel(info, own, east, south, corner, wave, amp, table, inner, g_own, g_east, g_south, g_corner):
    slots = wave.shape[0]
    quads_in = (own, east, south, corner)
    quads = (g_own, g_east, g_south, g_corner)
    clear(quads)

    def body(s, carry):
        low, right = wraps(own.shape[1:], info[0, 2 * s], info[0, 2 * s + 1])
        sr, si = pick(quads_in, 0, low, right), pick(quads_in, 1, low, right)
        wr, wi = wave[s, 0], wave[s, 1]
        fr, fi = forward(wr * sr - wi * si, wr * si + wi * sr, table)
        ratio = amp[s] * lax.rsqrt(jnp.maximum(fr * fr + fi * fi, 0.25)) - 1.0
        br, bi = backward(fr * ratio, fi * ratio, table)
        inner[s, 0] = sr * br + si * bi
        inner[s, 1] = sr * bi - si * br
        deposit(quads, 0, wr * br + wi * bi, low, right)
        deposit(quads, 1, wr * bi - wi * br, low, right)
        return carry

    lax.fori_loop(0, info[0, 2 * slots], body, 0)


def third_kernel(info, inner, shifted, phasor, table, g_own, g_east, g_south, g_corner):
    slots = inner.shape[0]
    quads = (g_own, g_east, g_south, g_corner)
    clear(quads)

    def body(s, carry):
        low, right = wraps(g_own.shape[1:], info[0, 2 * s], info[0, 2 * s + 1])
        tr, ti = forward(inner[s, 0], inner[s, 1], table)
        hr, hi = phasor[0], phasor[1]
        qr, qi = backward(tr * hr + ti * hi, ti * hr - tr * hi, table)
        pr, pi = shifted[s, 0], shifted[s, 1]
        deposit(quads, 0, pr * qr + pi * qi, low, right)
        deposit(quads, 1, pr * qi - pi * qr, low, right)
        return carry

    lax.fori_loop(0, info[0, 2 * slots], body, 0)


def call(kernel, shapes, *operands, microseconds=4):
    return pl.pallas_call(
        kernel,
        out_shape=[jax.ShapeDtypeStruct(s, F32) for s in shapes],
        in_specs=[SMEM] + [VMEM] * (len(operands) - 1),
        out_specs=[VMEM] * len(shapes),
        compiler_params=pltpu.CompilerParams(vmem_limit_bytes=32 << 20),
        cost_estimate=pl.CostEstimate(
            flops=microseconds * 10**9, bytes_accessed=microseconds * 10**6, transcendentals=0
        ),
    )(*operands)


def on_device(object_planes, probe, phase, coords, live, amplitude):
    width = probe.shape[-1]
    slots = coords.shape[2]
    tile = (width, width)
    pair = (2,) + tile
    table = jnp.asarray(transform_tables(width))
    order = jnp.asarray(order_table(width))

    own_info = jnp.concatenate([coords.reshape(1, 2 * slots), live.reshape(1, 1)], axis=1)
    first, second = object_planes[0:2], object_planes[2:4]
    east1 = from_behind(first, "tx", -1)
    south1 = from_behind(first, "ty", -1)
    east2 = from_behind(second, "tx", -1)
    south2 = from_behind(second, "ty", -1)
    corner1 = from_behind(east1, "ty", -1)
    corner2 = from_behind(east2, "ty", -1)
    info = jnp.concatenate(
        [own_info, from_behind(own_info, "tx", 1), from_behind(own_info, "ty", 1), from_diagonal(own_info, 1)]
    )

    phasor = jnp.stack([jnp.cos(phase), jnp.sin(phase)])
    shifted, amp, phasor = call(
        prep_kernel, [(slots,) + pair, (slots,) + tile, pair], own_info, probe, amplitude[0, 0], phasor, order
    )
    cover = call(cover_kernel, [tile], info, probe)[0]
    wave, *power = call(
        first_kernel,
        [(slots,) + pair] + [(1,) + tile] * 4,
        own_info, first, east1, south1, corner1, shifted, phasor, table,
    )
    inner, *grad2 = call(
        second_kernel,
        [(slots,) + pair] + [pair] * 4,
        own_info, second, east2, south2, corner2, wave, amp, table,
    )
    grad1 = call(third_kernel, [pair] * 4, own_info, inner, shifted, phasor, table)

    def gather_sums(own, east, south, corner):
        moved = from_behind(corner, "ty", 1)
        return own + from_behind(south, "ty", 1) + from_behind(east + moved, "tx", 1)

    sum_power = gather_sums(*power)
    sum2 = gather_sums(*grad2)
    sum1 = gather_sums(*grad1)
    return jnp.concatenate([first + sum1 / (cover + 1.0)[None], second + sum2 / (sum_power + 1.0)])


def solution(mesh):
    return jax.shard_map(
        on_device,
        mesh=mesh,
        in_specs=(
            P(None, ("groups", "ty"), "tx"),
            P(),
            P(),
            P(("groups", "ty"), "tx", None, None),
            P(("groups", "ty"), "tx"),
            P(("groups", "ty"), "tx", None, None, None),
        ),
        out_specs=P(None, ("groups", "ty"), "tx"),
        check_vma=False,
    )
```

profile of v0, /device:TPU:0, one launch (start us, length us, event | category | flops | bytes accessed | tf_op | source)
XLA Modules:
  0.0 133.7 jit_solution(1022623073267874)
XLA Ops:
  0.0 1.4 %fusion = (f32[2,256,256]{2,1,0:T(8,128)S(1)}, f32[2,256,256]{2,1,0:T(8,128)S(1)}) fusion(f32[4,256,256]{2,1,0:T(8,128)} %param.8), kind=kLoop, calls=%fused_computation.10 | loop fusion | bytes 2097152 | tf_op jit(solution)/shard_map/slice | solution.py:259
  1.4 1.3 collective-permute-start.3
  2.7 1.3 collective-permute-start
  4.0 1.3 collective-permute-start.4
  5.3 1.3 collective-permute-start.1
  6.6 0.0 copy-done.7
  6.6 0.1 copy.10
  6.7 0.1 reshape.4
  7.4 1.9 %cosine_bitcast_fusion = (f32[1,256,256]{2,1,0:T(8,128)S(1)}, f32[1,256,256]{2,1,0:T(8,128)S(1)}) fusion(f32[256,256]{1,0:T(8,128)} %param.10), kind=kLoop, calls=%fused_computation.6 | loop fusion | bytes 786432 | tf_op jit(solution)/shard_map/stack | solution.py:270
  9.3 9.9 %collective-permute-done.3.east = f32[2,256,256]{2,1,0:T(8,128)} collective-permute-done((f32[2,256,256]{2,1,0:T(8,128)S(1)}, f32[2,256,256]{2,1,0:T(8,128)}, u32[]{:S(2)}, u32[]{:S(2)}) %collective-permute-start.3) | collective-permute-done | bytes 524320 | tf_op jit(solution)/shard_map/ppermute | solution.py:22
  19.2 1.3 collective-permute-start.5
  20.5 0.1 pad_add_fusion.1.info
  20.6 8.9 %collective-permute-done.east = f32[2,256,256]{2,1,0:T(8,128)S(1)} collective-permute-done((f32[2,256,256]{2,1,0:T(8,128)S(1)}, f32[2,256,256]{2,1,0:T(8,128)S(1)}, u32[]{:S(2)}, u32[]{:S(2)}) %collective-permute-start) | collective-permute-done | bytes 524320 | tf_op jit(solution)/shard_map/ppermute | solution.py:22
  29.5 1.3 collective-permute-start.2
  30.8 0.0 copy-done
  30.8 0.0 copy-done.1
  30.8 0.0 copy-start.5
  30.8 1.0 copy-done.5
  31.9 4.2 %shard_map.82 = (f32[4,2,256,256]{3,2,1,0:T(8,128)S(1)}, f32[4,256,256]{2,1,0:T(8,128)S(1)}, f32[2,256,256]{2,1,0:T(8,128)S(1)}) custom-call(s32[1,9]{1,0:T(1,128)S(1)} %pad_add_fusion.1.info, f32[2,256,256]{2,1,0:T(8,128)S(1)} %copy-done.1, f32[4,256,256]{2,1,0:T(8,128)S(1)} %bitcast.7, f32[2,256,256]{2,1,0:T(8,128)S(1)} %pad_maximum_fusion.1.phasor, ...), custom_call_target="tpu_custom_call" | custom-call | flops 4000000000 | bytes 4000000 | tf_op jit(solution)/shard_map/pallas_call | solution.py:238
  36.1 0.0 collective-permute-done.4.south
  36.1 0.0 collective-permute-done.5.corner
  36.1 0.0 copy-done.4
  36.1 5.5 %shard_map.83 = (f32[4,2,256,256]{3,2,1,0:T(8,128)S(1)}, f32[1,256,256]{2,1,0:T(8,128)S(1)}, f32[1,256,256]{2,1,0:T(8,128)S(1)}, f32[1,256,256]{2,1,0:T(8,128)}, f32[1,256,256]{2,1,0:T(8,128)}) custom-call(s32[1,9]{1,0:T(1,128)S(1)} %pad_add_fusion.1.info, f32[2,256,256]{2,1,0:T(8,128)S(1)} %get-tuple-element.41.own, ...), custom_call_target="tpu_custom_call" | custom-call | flops 4000000000 | bytes 4000000 | tf_op jit(solution)/shard_map/pallas_call | solution.py:238
  41.5 0.0 collective-permute-done.1.south
  41.6 0.0 collective-permute-done.2.corner
  41.6 5.8 %shard_map.84 = (f32[4,2,256,256]{3,2,1,0:T(8,128)S(1)}, f32[2,256,256]{2,1,0:T(8,128)S(1)}, f32[2,256,256]{2,1,0:T(8,128)S(1)}, f32[2,256,256]{2,1,0:T(8,128)S(1)}, f32[2,256,256]{2,1,0:T(8,128)}) custom-call(s32[1,9]{1,0:T(1,128)S(1)} %pad_add_fusion.1.info, f32[2,256,256]{2,1,0:T(8,128)S(1)} %get-tuple-element.42.own, ...), custom_call_target="tpu_custom_call" | custom-call | flops 4000000000 | bytes 4000000 | tf_op jit(solution)/shard_map/pallas_call | solution.py:238
  47.3 2.1 %collective-permute-start.13 = (f32[2,256,256]{2,1,0:T(8,128)}, f32[2,256,256]{2,1,0:T(8,128)}, u32[]{:S(2)}, u32[]{:S(2)}) collective-permute-start(f32[2,256,256]{2,1,0:T(8,128)} %get-tuple-element.34), channel_id=1, source_target_pairs={{0,4},{4,8},{8,12},{1,5},{5,9},{9,13},{2,6},{6,10},{10,14},{3,7},{... | collective-permute-start | bytes 1572872 | tf_op jit(solution)/shard_map/ppermute | solution.py:22
  49.4 4.7 %shard_map.85 = (f32[2,256,256]{2,1,0:T(8,128)S(1)}, f32[2,256,256]{2,1,0:T(8,128)S(1)}, f32[2,256,256]{2,1,0:T(8,128)S(1)}, f32[2,256,256]{2,1,0:T(8,128)}) custom-call(s32[1,9]{1,0:T(1,128)S(1)} %pad_add_fusion.1.info, f32[4,2,256,256]{3,2,1,0:T(8,128)S(1)} %get-tuple-element.26.inner, f32[4,2,256,256]{3,2,1,0:T(8,128)S(1)} %get-tuple-element.22.shifted, ...), custom_call_target="tpu_custom_call" | custom-call | flops 4000000000 | bytes 4000000 | tf_op jit(solution)/shard_map/pallas_call | solution.py:238
  54.2 0.0 copy-done.2
  54.2 0.8 copy-done.3
  55.0 2.1 %collective-permute-start.7 = (f32[2,256,256]{2,1,0:T(8,128)}, f32[2,256,256]{2,1,0:T(8,128)}, u32[]{:S(2)}, u32[]{:S(2)}) collective-permute-start(f32[2,256,256]{2,1,0:T(8,128)} %get-tuple-element.30), channel_id=1, source_target_pairs={{0,4},{4,8},{8,12},{1,5},{5,9},{9,13},{2,6},{6,10},{10,14},{3,7},{... | collective-permute-start | bytes 1572872 | tf_op jit(solution)/shard_map/ppermute | solution.py:22
  57.0 1.3 collective-permute-start.16
  58.4 2.0 %collective-permute-start.15 = (f32[1,256,256]{2,1,0:T(8,128)}, f32[1,256,256]{2,1,0:T(8,128)}, u32[]{:S(2)}, u32[]{:S(2)}) collective-permute-start(f32[1,256,256]{2,1,0:T(8,128)} %get-tuple-element.36), channel_id=1, source_target_pairs={{0,4},{4,8},{8,12},{1,5},{5,9},{9,13},{2,6},{6,10},{10,14},{3,7},{... | collective-permute-start | bytes 786440 | tf_op jit(solution)/shard_map/ppermute | solution.py:22
  60.3 1.3 collective-permute-start.10
  61.6 0.8 collective-permute-done.10
  62.4 5.5 %collective-permute-start.11 = (s32[1,9]{1,0:T(1,128)S(1)}, s32[1,9]{1,0:T(1,128)S(1)}, u32[]{:S(2)}, u32[]{:S(2)}) collective-permute-start(s32[1,9]{1,0:T(1,128)S(1)} %pad_add_fusion.1.info), channel_id=1, source_target_pairs={{0,5},{1,6},{2,7},{4,9},{5,10},{6,11},{8,13},{9,14},{10,15},{16,21... | collective-permute-start | bytes 116 | tf_op jit(solution)/shard_map/ppermute | solution.py:33
  67.9 1.3 collective-permute-done.11
  69.2 22.4 %collective-permute-start.9 = (s32[1,9]{1,0:T(1,128)S(1)}, s32[1,9]{1,0:T(1,128)S(1)}, u32[]{:S(2)}, u32[]{:S(2)}) collective-permute-start(s32[1,9]{1,0:T(1,128)S(1)} %pad_add_fusion.1.info), channel_id=1, source_target_pairs={{0,1},{1,2},{2,3},{4,5},{5,6},{6,7},{8,9},{9,10},{10,11},{12,13},{... | collective-permute-start | bytes 116 | tf_op jit(solution)/shard_map/ppermute | solution.py:22
  91.6 1.3 collective-permute-done.9
  92.9 0.1 pad_add_fusion.info
  93.0 2.8 %collective-permute-start.6 = (f32[2,256,256]{2,1,0:T(8,128)}, f32[2,256,256]{2,1,0:T(8,128)S(1)}, u32[]{:S(2)}, u32[]{:S(2)}) collective-permute-start(f32[2,256,256]{2,1,0:T(8,128)} %copy-done.3), channel_id=1, source_target_pairs={{0,4},{4,8},{8,12},{1,5},{5,9},{9,13},{2,6},{6,10},{10,14},{3,7},{... | collective-permute-start | bytes 1572872 | tf_op jit(solution)/shard_map/ppermute | solution.py:22
  95.8 0.0 collective-permute-done.16
  95.8 1.9 %collective-permute-start.12 = (f32[2,256,256]{2,1,0:T(8,128)}, f32[2,256,256]{2,1,0:T(8,128)S(1)}, u32[]{:S(2)}, u32[]{:S(2)}) collective-permute-start(f32[2,256,256]{2,1,0:T(8,128)} %copy-done.2), channel_id=1, source_target_pairs={{0,4},{4,8},{8,12},{1,5},{5,9},{9,13},{2,6},{6,10},{10,14},{3,7},{... | collective-permute-start | bytes 1572872 | tf_op jit(solution)/shard_map/ppermute | solution.py:22
  97.8 0.0 collective-permute-done.13
  97.8 6.5 %collective-permute-start.17 = (f32[1,256,256]{2,1,0:T(8,128)S(1)}, f32[1,256,256]{2,1,0:T(8,128)S(1)}, u32[]{:S(2)}, u32[]{:S(2)}) collective-permute-start(f32[1,256,256]{2,1,0:T(8,128)S(1)} %add.55), channel_id=1, source_target_pairs={{0,1},{1,2},{2,3},{4,5},{5,6},{6,7},{8,9},{9,10},{10,11},{12,13},{... | collective-permute-start | bytes 786440 | tf_op jit(solution)/shard_map/ppermute | solution.py:22
  104.3 1.1 add.52
  105.4 0.0 collective-permute-done.7
  105.4 4.2 %collective-permute-start.14 = (f32[2,256,256]{2,1,0:T(8,128)S(1)}, f32[2,256,256]{2,1,0:T(8,128)S(1)}, u32[]{:S(2)}, u32[]{:S(2)}) collective-permute-start(f32[2,256,256]{2,1,0:T(8,128)S(1)} %add.52), channel_id=1, source_target_pairs={{0,1},{1,2},{2,3},{4,5},{5,6},{6,7},{8,9},{9,10},{10,11},{12,13},{... | collective-permute-start | bytes 1572872 | tf_op jit(solution)/shard_map/ppermute | solution.py:22
  109.6 1.1 add.46
  110.7 0.0 copy-start.8
  110.7 0.0 collective-permute-done.15
  110.7 2.1 %collective-permute-start.8 = (f32[2,256,256]{2,1,0:T(8,128)S(1)}, f32[2,256,256]{2,1,0:T(8,128)S(1)}, u32[]{:S(2)}, u32[]{:S(2)}) collective-permute-start(f32[2,256,256]{2,1,0:T(8,128)S(1)} %add.46), channel_id=1, source_target_pairs={{0,1},{1,2},{2,3},{4,5},{5,6},{6,7},{8,9},{9,10},{10,11},{12,13},{... | collective-permute-start | bytes 1572872 | tf_op jit(solution)/shard_map/ppermute | solution.py:22
  112.8 1.0 shard_map.86
  113.8 0.0 copy-start.6
  113.8 0.0 collective-permute-done.17
  113.8 1.1 add_bitcast_fusion
  114.9 0.0 collective-permute-done.6
  114.9 0.0 collective-permute-done.12
  114.9 6.9 %collective-permute-done.14 = f32[2,256,256]{2,1,0:T(8,128)S(1)} collective-permute-done((f32[2,256,256]{2,1,0:T(8,128)S(1)}, f32[2,256,256]{2,1,0:T(8,128)S(1)}, u32[]{:S(2)}, u32[]{:S(2)}) %collective-permute-start.14) | collective-permute-done | bytes 524320 | tf_op jit(solution)/shard_map/ppermute | solution.py:22
  121.9 10.5 %collective-permute-done.8 = f32[2,256,256]{2,1,0:T(8,128)S(1)} collective-permute-done((f32[2,256,256]{2,1,0:T(8,128)S(1)}, f32[2,256,256]{2,1,0:T(8,128)S(1)}, u32[]{:S(2)}, u32[]{:S(2)}) %collective-permute-start.8) | collective-permute-done | bytes 524320 | tf_op jit(solution)/shard_map/ppermute | solution.py:22
  132.4 0.0 copy-done.8
  132.4 0.3 divide_add_fusion.1
  132.7 0.0 copy-start.9
  132.8 1.0 copy-done.9
  (11 shorter events, 0.1 us)
Async XLA Ops:
  0.0 6.6 %copy-start.7 = (s32[1,1,4,2]{2,3,1,0:T(2,128)S(1)}, s32[1,1,4,2]{2,3,1,0:T(2,128)}, u32[]{:S(2)}) copy-start(s32[1,1,4,2]{2,3,1,0:T(2,128)} %param.11) | copy-start | bytes 100
  0.0 30.8 %copy-start = (f32[1,1,4,256,256]{4,3,2,1,0:T(8,128)S(1)}, f32[1,1,4,256,256]{4,3,2,1,0:T(8,128)}, u32[]{:S(2)}) copy-start(f32[1,1,4,256,256]{4,3,2,1,0:T(8,128)} %param.13) | copy-start | bytes 3145732
  0.0 30.8 %copy-start.1 = (f32[2,256,256]{2,1,0:T(8,128)S(1)}, f32[2,256,256]{2,1,0:T(8,128)}, u32[]{:S(2)}) copy-start(f32[2,256,256]{2,1,0:T(8,128)} %probe.3) | copy-start | bytes 1572868
  1.4 17.8 %collective-permute-start.3 = (f32[2,256,256]{2,1,0:T(8,128)S(1)}, f32[2,256,256]{2,1,0:T(8,128)}, u32[]{:S(2)}, u32[]{:S(2)}) collective-permute-start(f32[2,256,256]{2,1,0:T(8,128)S(1)} %get-tuple-element.41.own), channel_id=1, source_target_pairs={{1,0},{2,1},{3,2},{5,4},{6,5},{7,6},{9,8},{10,9},{11,10},{13,12},{... | collective-permute-start | bytes 1572872 | tf_op jit(solution)/shard_map/ppermute | solution.py:22
  2.7 26.8 %collective-permute-start = (f32[2,256,256]{2,1,0:T(8,128)S(1)}, f32[2,256,256]{2,1,0:T(8,128)S(1)}, u32[]{:S(2)}, u32[]{:S(2)}) collective-permute-start(f32[2,256,256]{2,1,0:T(8,128)S(1)} %get-tuple-element.42.own), channel_id=1, source_target_pairs={{1,0},{2,1},{3,2},{5,4},{6,5},{7,6},{9,8},{10,9},{11,10},{13,12},{... | collective-permute-start | bytes 1572872 | tf_op jit(solution)/shard_map/ppermute | solution.py:22
  4.0 32.1 %collective-permute-start.4 = (f32[2,256,256]{2,1,0:T(8,128)S(1)}, f32[2,256,256]{2,1,0:T(8,128)}, u32[]{:S(2)}, u32[]{:S(2)}) collective-permute-start(f32[2,256,256]{2,1,0:T(8,128)S(1)} %get-tuple-element.41.own), channel_id=1, source_target_pairs={{4,0},{8,4},{12,8},{5,1},{9,5},{13,9},{6,2},{10,6},{14,10},{7,3},{... | collective-permute-start | bytes 1572872 | tf_op jit(solution)/shard_map/ppermute | solution.py:22
  5.3 36.2 %collective-permute-start.1 = (f32[2,256,256]{2,1,0:T(8,128)S(1)}, f32[2,256,256]{2,1,0:T(8,128)}, u32[]{:S(2)}, u32[]{:S(2)}) collective-permute-start(f32[2,256,256]{2,1,0:T(8,128)S(1)} %get-tuple-element.42.own), channel_id=1, source_target_pairs={{4,0},{8,4},{12,8},{5,1},{9,5},{13,9},{6,2},{10,6},{14,10},{7,3},{... | collective-permute-start | bytes 1572872 | tf_op jit(solution)/shard_map/ppermute | solution.py:22
  19.2 16.9 %collective-permute-start.5 = (f32[2,256,256]{2,1,0:T(8,128)}, f32[2,256,256]{2,1,0:T(8,128)S(1)}, u32[]{:S(2)}, u32[]{:S(2)}) collective-permute-start(f32[2,256,256]{2,1,0:T(8,128)} %collective-permute-done.3.east), channel_id=1, source_target_pairs={{4,0},{8,4},{12,8},{5,1},{9,5},{13,9},{6,2},{10,6},{14,10},{7,3},{... | collective-permute-start | bytes 1572872 | tf_op jit(solution)/shard_map/ppermute | solution.py:22
  29.5 12.1 %collective-permute-start.2 = (f32[2,256,256]{2,1,0:T(8,128)S(1)}, f32[2,256,256]{2,1,0:T(8,128)S(1)}, u32[]{:S(2)}, u32[]{:S(2)}) collective-permute-start(f32[2,256,256]{2,1,0:T(8,128)S(1)} %collective-permute-done.east), channel_id=1, source_target_pairs={{4,0},{8,4},{12,8},{5,1},{9,5},{13,9},{6,2},{10,6},{14,10},{7,3},{... | collective-permute-start | bytes 1572872 | tf_op jit(solution)/shard_map/ppermute | solution.py:22
  30.8 1.0 copy-start.5
  31.9 4.2 %copy-start.4 = (bf16[8,256,256]{2,1,0:T(8,128)(2,1)S(1)}, bf16[8,256,256]{2,1,0:T(8,128)(2,1)}, u32[]{:S(2)}) copy-start(bf16[8,256,256]{2,1,0:T(8,128)(2,1)} %constant.2.clone.table) | copy-start | bytes 3145732
  47.3 6.8 %copy-start.2 = (f32[2,256,256]{2,1,0:T(8,128)}, f32[2,256,256]{2,1,0:T(8,128)S(1)}, u32[]{:S(2)}) copy-start(f32[2,256,256]{2,1,0:T(8,128)S(1)} %get-tuple-element.32) | copy-start | bytes 1572868
  47.3 50.4 %collective-permute-start.13 = (f32[2,256,256]{2,1,0:T(8,128)}, f32[2,256,256]{2,1,0:T(8,128)}, u32[]{:S(2)}, u32[]{:S(2)}) collective-permute-start(f32[2,256,256]{2,1,0:T(8,128)} %get-tuple-element.34), channel_id=1, source_target_pairs={{0,4},{4,8},{8,12},{1,5},{5,9},{9,13},{2,6},{6,10},{10,14},{3,7},{... | collective-permute-start | bytes 1572872 | tf_op jit(solution)/shard_map/ppermute | solution.py:22
  54.2 0.8 copy-start.3
  55.0 50.4 %collective-permute-start.7 = (f32[2,256,256]{2,1,0:T(8,128)}, f32[2,256,256]{2,1,0:T(8,128)}, u32[]{:S(2)}, u32[]{:S(2)}) collective-permute-start(f32[2,256,256]{2,1,0:T(8,128)} %get-tuple-element.30), channel_id=1, source_target_pairs={{0,4},{4,8},{8,12},{1,5},{5,9},{9,13},{2,6},{6,10},{10,14},{3,7},{... | collective-permute-start | bytes 1572872 | tf_op jit(solution)/shard_map/ppermute | solution.py:22
  57.0 38.7 %collective-permute-start.16 = (f32[1,256,256]{2,1,0:T(8,128)}, f32[1,256,256]{2,1,0:T(8,128)S(1)}, u32[]{:S(2)}, u32[]{:S(2)}) collective-permute-start(f32[1,256,256]{2,1,0:T(8,128)} %get-tuple-element.38), channel_id=1, source_target_pairs={{0,4},{4,8},{8,12},{1,5},{5,9},{9,13},{2,6},{6,10},{10,14},{3,7},{... | collective-permute-start | bytes 786440 | tf_op jit(solution)/shard_map/ppermute | solution.py:22
  58.4 52.3 %collective-permute-start.15 = (f32[1,256,256]{2,1,0:T(8,128)}, f32[1,256,256]{2,1,0:T(8,128)}, u32[]{:S(2)}, u32[]{:S(2)}) collective-permute-start(f32[1,256,256]{2,1,0:T(8,128)} %get-tuple-element.36), channel_id=1, source_target_pairs={{0,4},{4,8},{8,12},{1,5},{5,9},{9,13},{2,6},{6,10},{10,14},{3,7},{... | collective-permute-start | bytes 786440 | tf_op jit(solution)/shard_map/ppermute | solution.py:22
  60.3 2.1 %collective-permute-start.10 = (s32[1,9]{1,0:T(1,128)S(1)}, s32[1,9]{1,0:T(1,128)S(1)}, u32[]{:S(2)}, u32[]{:S(2)}) collective-permute-start(s32[1,9]{1,0:T(1,128)S(1)} %pad_add_fusion.1.info), channel_id=1, source_target_pairs={{0,4},{4,8},{8,12},{1,5},{5,9},{9,13},{2,6},{6,10},{10,14},{3,7},{... | collective-permute-start | bytes 116 | tf_op jit(solution)/shard_map/ppermute | solution.py:22
  62.4 6.8 %collective-permute-start.11 = (s32[1,9]{1,0:T(1,128)S(1)}, s32[1,9]{1,0:T(1,128)S(1)}, u32[]{:S(2)}, u32[]{:S(2)}) collective-permute-start(s32[1,9]{1,0:T(1,128)S(1)} %pad_add_fusion.1.info), channel_id=1, source_target_pairs={{0,5},{1,6},{2,7},{4,9},{5,10},{6,11},{8,13},{9,14},{10,15},{16,21... | collective-permute-start | bytes 116 | tf_op jit(solution)/shard_map/ppermute | solution.py:33
  69.2 23.7 %collective-permute-start.9 = (s32[1,9]{1,0:T(1,128)S(1)}, s32[1,9]{1,0:T(1,128)S(1)}, u32[]{:S(2)}, u32[]{:S(2)}) collective-permute-start(s32[1,9]{1,0:T(1,128)S(1)} %pad_add_fusion.1.info), channel_id=1, source_target_pairs={{0,1},{1,2},{2,3},{4,5},{5,6},{6,7},{8,9},{9,10},{10,11},{12,13},{... | collective-permute-start | bytes 116 | tf_op jit(solution)/shard_map/ppermute | solution.py:22
  93.0 21.9 %collective-permute-start.6 = (f32[2,256,256]{2,1,0:T(8,128)}, f32[2,256,256]{2,1,0:T(8,128)S(1)}, u32[]{:S(2)}, u32[]{:S(2)}) collective-permute-start(f32[2,256,256]{2,1,0:T(8,128)} %copy-done.3), channel_id=1, source_target_pairs={{0,4},{4,8},{8,12},{1,5},{5,9},{9,13},{2,6},{6,10},{10,14},{3,7},{... | collective-permute-start | bytes 1572872 | tf_op jit(solution)/shard_map/ppermute | solution.py:22
  95.8 19.1 %collective-permute-start.12 = (f32[2,256,256]{2,1,0:T(8,128)}, f32[2,256,256]{2,1,0:T(8,128)S(1)}, u32[]{:S(2)}, u32[]{:S(2)}) collective-permute-start(f32[2,256,256]{2,1,0:T(8,128)} %copy-done.2), channel_id=1, source_target_pairs={{0,4},{4,8},{8,12},{1,5},{5,9},{9,13},{2,6},{6,10},{10,14},{3,7},{... | collective-permute-start | bytes 1572872 | tf_op jit(solution)/shard_map/ppermute | solution.py:22
  97.8 16.0 %collective-permute-start.17 = (f32[1,256,256]{2,1,0:T(8,128)S(1)}, f32[1,256,256]{2,1,0:T(8,128)S(1)}, u32[]{:S(2)}, u32[]{:S(2)}) collective-permute-start(f32[1,256,256]{2,1,0:T(8,128)S(1)} %add.55), channel_id=1, source_target_pairs={{0,1},{1,2},{2,3},{4,5},{5,6},{6,7},{8,9},{9,10},{10,11},{12,13},{... | collective-permute-start | bytes 786440 | tf_op jit(solution)/shard_map/ppermute | solution.py:22
  105.4 16.5 %collective-permute-start.14 = (f32[2,256,256]{2,1,0:T(8,128)S(1)}, f32[2,256,256]{2,1,0:T(8,128)S(1)}, u32[]{:S(2)}, u32[]{:S(2)}) collective-permute-start(f32[2,256,256]{2,1,0:T(8,128)S(1)} %add.52), channel_id=1, source_target_pairs={{0,1},{1,2},{2,3},{4,5},{5,6},{6,7},{8,9},{9,10},{10,11},{12,13},{... | collective-permute-start | bytes 1572872 | tf_op jit(solution)/shard_map/ppermute | solution.py:22
  110.7 21.7 %copy-start.8 = (f32[4,256,256]{2,1,0:T(8,128)S(1)}, f32[4,256,256]{2,1,0:T(8,128)}, u32[]{:S(2)}) copy-start(f32[4,256,256]{2,1,0:T(8,128)} %custom-call) | copy-start | bytes 3145732
  110.7 21.7 %collective-permute-start.8 = (f32[2,256,256]{2,1,0:T(8,128)S(1)}, f32[2,256,256]{2,1,0:T(8,128)S(1)}, u32[]{:S(2)}, u32[]{:S(2)}) collective-permute-start(f32[2,256,256]{2,1,0:T(8,128)S(1)} %add.46), channel_id=1, source_target_pairs={{0,1},{1,2},{2,3},{4,5},{5,6},{6,7},{8,9},{9,10},{10,11},{12,13},{... | collective-permute-start | bytes 1572872 | tf_op jit(solution)/shard_map/ppermute | solution.py:22
  113.8 18.6 %copy-start.6 = (f32[4,256,256]{2,1,0:T(8,128)S(1)}, f32[4,256,256]{2,1,0:T(8,128)}, u32[]{:S(2)}) copy-start(f32[4,256,256]{2,1,0:T(8,128)} %param.8) | copy-start | bytes 3145732
  132.7 1.0 copy-start.9
where the time goes:
time: 133 us; the launch traced here: 134 us
  starting transfers between devices  61.8 us (46%)
  waiting for transfers between devices  39.6 us (30%)
  Pallas kernels  21.2 us (16%)
  local copies, waits for them, and re-layouts  6.26 us (5%)
  other arithmetic  3.87 us (3%)
    ppermute x17, starting transfers between devices, from_behind(): return lax.ppermute(block, axis, route)  56.3 us
    ppermute x17, waiting for transfers between devices, from_behind(): return lax.ppermute(block, axis, route)  38.4 us
    pallas_call x5, Pallas kernels, call(): pl.pallas_call(kernel, out_shape=[jax.ShapeDtypeStruct(s, F32) for s in s...  21.2 us
    ppermute x1, starting transfers between devices, from_diagonal(): return lax.ppermute(block, ('ty', 'tx'), route)  5.5 us
    unnamed x21, local copies, waits for them, and re-layouts  2.92 us
  transfers between devices with their start and end apart: 18, of which 7 were waited for; matrix products, arithmetic and copies ran while one was open for 4% of the time, Pallas kernels for 12%

commit v1 on v0

v1 whole, which is shorter than its diff:
```python
import math

import jax
import jax.numpy as jnp
import ml_dtypes
import numpy as np
from jax import lax
from jax.experimental import pallas as pl
from jax.experimental.pallas import tpu as pltpu
from jax.sharding import PartitionSpec as P

F32 = jnp.float32
BF16 = jnp.bfloat16
VMEM = pl.BlockSpec(memory_space=pltpu.VMEM)
SMEM = pl.BlockSpec(memory_space=pltpu.SMEM)


def from_behind(block, axis, distance):
    devices = range(lax.axis_size(axis))
    route = [(i - distance, i) for i in devices if i - distance in devices]
    return lax.ppermute(block, axis, route)


def transform_tables(width):
    half = width // 2
    n = np.arange(half)[:, None]
    k = np.arange(half)[None, :]
    out = []
    for odd in (0, 1):
        angle = -2.0 * math.pi * ((n * (2 * k + odd)) % width) / width
        wr, wi = np.cos(angle) / math.sqrt(width), np.sin(angle) / math.sqrt(width)
        real = np.block([[wr, wi], [-wi, wr]])
        head = real.astype(ml_dtypes.bfloat16)
        tail = (real - head.astype(np.float64)).astype(ml_dtypes.bfloat16)
        out += [head, tail]
    out += [np.ascontiguousarray(m.T) for m in out]
    return np.stack(out)


def order_table(width):
    half = width // 2
    table = np.zeros((2, width, width), ml_dtypes.bfloat16)
    source = np.concatenate([np.arange(0, width, 2), np.arange(1, width, 2)])
    table[0, np.arange(width), source] = 1.0
    table[1] = table[0].T
    return table


def split(x):
    head = x.astype(BF16)
    return head, (x - head.astype(F32)).astype(BF16)


def mm(a, b):
    return jnp.dot(a, b, preferred_element_type=F32)


def right_mul(x, table, at):
    head, tail = split(x)
    return mm(head, table[at]) + mm(tail, table[at]) + mm(head, table[at + 1])


def left_mul(x, table, at):
    head, tail = split(x)
    return mm(table[at], head) + mm(table[at], tail) + mm(table[at + 1], head)


def stack_rows(blocks):
    return jnp.concatenate(blocks, axis=0)


def stack_cols(blocks):
    return jnp.concatenate(blocks, axis=1)


def forward(waves, table):
    half = waves[0][0].shape[0] // 2
    steps = []
    for xr, xi in waves:
        sums = stack_rows([xr[:half] + xr[half:], xi[:half] + xi[half:]])
        diffs = stack_rows([xr[:half] - xr[half:], xi[:half] - xi[half:]])
        steps.append((left_mul(sums, table, 4), left_mul(diffs, table, 6)))
    out = []
    for even, odd in steps:
        yr = stack_rows([even[:half], odd[:half]])
        yi = stack_rows([even[half:], odd[half:]])
        sums = stack_cols([yr[:, :half] + yr[:, half:], yi[:, :half] + yi[:, half:]])
        diffs = stack_cols([yr[:, :half] - yr[:, half:], yi[:, :half] - yi[:, half:]])
        out.append((right_mul(sums, table, 0), right_mul(diffs, table, 2)))
    return [
        (stack_cols([even[:, :half], odd[:, :half]]), stack_cols([even[:, half:], odd[:, half:]]))
        for even, odd in out
    ]


def backward(waves, table):
    half = waves[0][0].shape[0] // 2
    steps = []
    for xr, xi in waves:
        even = left_mul(stack_rows([xr[:half], xi[:half]]), table, 0)
        odd = left_mul(stack_rows([xr[half:], xi[half:]]), table, 2)
        steps.append((even, odd))
    out = []
    for even, odd in steps:
        yr = stack_rows([even[:half] + odd[:half], even[:half] - odd[:half]])
        yi = stack_rows([even[half:] + odd[half:], even[half:] - odd[half:]])
        even = right_mul(stack_cols([yr[:, :half], yi[:, :half]]), table, 4)
        odd = right_mul(stack_cols([yr[:, half:], yi[:, half:]]), table, 6)
        out.append((even, odd))
    return [
        tuple(
            stack_cols([even[:, part] + odd[:, part], even[:, part] - odd[:, part]])
            for part in (slice(0, half), slice(half, None))
        )
        for even, odd in out
    ]


class Window:
    def __init__(self, info, tile, slot, shape):
        slots = (info.shape[1] - 1) // 2
        rows = lax.broadcasted_iota(jnp.int32, shape, 0)
        cols = lax.broadcasted_iota(jnp.int32, shape, 1)
        self.low = rows < info[tile, 2 * slot]
        self.right = cols < info[tile, 2 * slot + 1]
        mine = self.right if tile else ~self.right
        mine = mine & (slot < info[tile, 2 * slots])
        self.keep_up = mine & ~self.low
        self.keep_low = mine & self.low

    def pick(self, quads, plane):
        own, east, south, corner = (q[plane] for q in quads)
        return jnp.where(self.low, jnp.where(self.right, corner, south), jnp.where(self.right, east, own))

    def deposit(self, up, low, plane, value):
        up[plane] += jnp.where(self.keep_up, value, 0.0)
        low[plane] += jnp.where(self.keep_low, value, 0.0)


def each_group(info, tile, body):
    slots = (info.shape[1] - 1) // 2
    group = 2 if slots % 2 == 0 else 1

    def step(g, carry):
        body([g * group + j for j in range(group)])
        return carry

    lax.fori_loop(0, (info[tile, 2 * slots] + group - 1) // group, step, 0)


def clear(*refs):
    for ref in refs:
        ref[...] = jnp.zeros_like(ref)


def prep_kernel(info, amp, phasor, order, amp_out, phasor_out):
    slots = amp.shape[0]

    def reorder(x):
        head, tail = split(x)
        once = mm(head, order[1]) + mm(tail, order[1])
        head, tail = split(once)
        return mm(order[0], head) + mm(order[0], tail)

    for part in range(2):
        phasor_out[part] = reorder(phasor[part])

    def reorder_amp(s, carry):
        amp_out[s] = reorder(amp[s])
        return carry

    lax.fori_loop(0, info[0, 2 * slots], reorder_amp, 0)


def shift_kernel(info, probe, shifted):
    slots = shifted.shape[1]
    for tile in range(2):

        def body(s, carry, tile=tile):
            top, left = info[tile, 2 * s], info[tile, 2 * s + 1]
            for part in range(2):
                shifted[tile, s, part] = pltpu.roll(pltpu.roll(probe[part], top, 0), left, 1)
            return carry

        lax.fori_loop(0, info[tile, 2 * slots], body, 0)


def first_kernel(
    info, own, east, south, corner, west, west_south, shifted, phasor, table, wave, up, low
):
    clear(up, low)
    shape = own.shape[1:]
    for tile, quads in ((0, (own, east, south, corner)), (1, (west, own, west_south, south))):

        def body(slots, tile=tile, quads=quads):
            windows = [Window(info, tile, s, shape) for s in slots]
            waves = []
            for s, w in zip(slots, windows):
                fr, fi = w.pick(quads, 0), w.pick(quads, 1)
                pr, pi = shifted[tile, s, 0], shifted[tile, s, 1]
                w.deposit(up, low, 1, pr * pr + pi * pi)
                waves.append((pr * fr - pi * fi, pr * fi + pi * fr))
            waves = forward(waves, table)
            hr, hi = phasor[0], phasor[1]
            waves = backward([(ur * hr - ui * hi, ur * hi + ui * hr) for ur, ui in waves], table)
            for s, w, (wr, wi) in zip(slots, windows, waves):
                wave[tile, s, 0] = wr
                wave[tile, s, 1] = wi
                w.deposit(up, low, 0, wr * wr + wi * wi)

        each_group(info, tile, body)


def second_step(info, tile, slots, quads, wave, amp, table, inner, up, low):
    shape = quads[0].shape[1:]
    windows = [Window(info, tile, s, shape) for s in slots]
    waves = []
    for s, w in zip(slots, windows):
        sr, si = w.pick(quads, 0), w.pick(quads, 1)
        wr, wi = wave[tile, s, 0], wave[tile, s, 1]
        waves.append((wr * sr - wi * si, wr * si + wi * sr))
    scaled = []
    for s, (fr, fi) in zip(slots, forward(waves, table)):
        ratio = amp[s] * lax.rsqrt(jnp.maximum(fr * fr + fi * fi, 0.25)) - 1.0
        scaled.append((fr * ratio, fi * ratio))
    for s, w, (br, bi) in zip(slots, windows, backward(scaled, table)):
        sr, si = w.pick(quads, 0), w.pick(quads, 1)
        wr, wi = wave[tile, s, 0], wave[tile, s, 1]
        inner[s, 0] = sr * br + si * bi
        inner[s, 1] = sr * bi - si * br
        w.deposit(up, low, 0, wr * br + wi * bi)
        w.deposit(up, low, 1, wr * bi - wi * br)


def third_step(info, tile, slots, inner, shifted, phasor, table, up, low):
    shape = up.shape[1:]
    waves = forward([(inner[s, 0], inner[s, 1]) for s in slots], table)
    hr, hi = phasor[0], phasor[1]
    waves = backward([(tr * hr + ti * hi, ti * hr - tr * hi) for tr, ti in waves], table)
    for s, (qr, qi) in zip(slots, waves):
        w = Window(info, tile, s, shape)
        pr, pi = shifted[tile, s, 0], shifted[tile, s, 1]
        w.deposit(up, low, 0, pr * qr + pi * qi)
        w.deposit(up, low, 1, pr * qi - pi * qr)


def own_kernel(
    info, own, east, south, corner, wave, amp, shifted, phasor, table, up2, low2, up1, low1, inner
):
    clear(up2, low2, up1, low1)
    quads = (own, east, south, corner)

    def body(slots):
        second_step(info, 0, slots, quads, wave, amp, table, inner, up2, low2)
        third_step(info, 0, slots, inner, shifted, phasor, table, up1, low1)

    each_group(info, 0, body)


def west_second_kernel(
    info, own, south, west, west_south, wave, amp, table, up_in, low_in, inner, up, low
):
    up[...] = up_in[...]
    low[...] = low_in[...]
    quads = (west, own, west_south, south)
    each_group(
        info, 1, lambda slots: second_step(info, 1, slots, quads, wave, amp, table, inner, up, low)
    )


def west_third_kernel(info, inner, shifted, phasor, table, up_in, low_in, up, low):
    up[...] = up_in[...]
    low[...] = low_in[...]
    each_group(
        info, 1, lambda slots: third_step(info, 1, slots, inner, shifted, phasor, table, up, low)
    )


def call(kernel, shapes, *operands, scratch=(), microseconds=4):
    return pl.pallas_call(
        kernel,
        out_shape=[pltpu.VMEM(s, F32) for s in shapes],
        in_specs=[SMEM] + [VMEM] * (len(operands) - 1),
        out_specs=[VMEM] * len(shapes),
        scratch_shapes=[pltpu.VMEM(s, F32) for s in scratch],
        compiler_params=pltpu.CompilerParams(vmem_limit_bytes=20 << 20),
        cost_estimate=pl.CostEstimate(
            flops=microseconds * 10**9, bytes_accessed=microseconds * 10**6, transcendentals=0
        ),
    )(*operands)


def on_device(object_planes, probe, phase, coords, live, amplitude):
    width = probe.shape[-1]
    slots = coords.shape[2]
    tile = (width, width)
    pair = (2,) + tile
    table = jnp.asarray(transform_tables(width))
    order = jnp.asarray(order_table(width))

    own_info = jnp.concatenate([coords.reshape(1, 2 * slots), live.reshape(1, 1)], axis=1)
    first, second = object_planes[0:2], object_planes[2:4]
    info = jnp.concatenate([own_info, from_behind(own_info, "tx", 1)])
    east1 = from_behind(first, "tx", -1)
    west1 = from_behind(first, "tx", 1)
    south1 = from_behind(first, "ty", -1)
    east2 = from_behind(second, "tx", -1)
    west2 = from_behind(second, "tx", 1)
    south2 = from_behind(second, "ty", -1)
    phasor = jnp.stack([jnp.cos(phase), jnp.sin(phase)])
    amp, phasor = call(prep_kernel, [(slots,) + tile, pair], own_info, amplitude[0, 0], phasor, order)
    amp_west = from_behind(amp, "tx", 1)
    shifted = call(shift_kernel, [(2, slots) + pair], info, probe)[0]

    corner1 = from_behind(east1, "ty", -1)
    west_south1 = from_behind(west1, "ty", -1)
    corner2 = from_behind(east2, "ty", -1)
    west_south2 = from_behind(west2, "ty", -1)

    wave, power_up, power_low = call(
        first_kernel,
        [(2, slots) + pair, pair, pair],
        info, first, east1, south1, corner1, west1, west_south1, shifted, phasor, table,
        microseconds=10,
    )
    power_moved = from_behind(power_low, "ty", 1)
    up2, low2, up1, low1 = call(
        own_kernel,
        [pair] * 4,
        info, second, east2, south2, corner2, wave, amp, shifted, phasor, table,
        scratch=[(slots,) + pair], microseconds=10,
    )
    inner, up2, low2 = call(
        west_second_kernel,
        [(slots,) + pair, pair, pair],
        info, second, south2, west2, west_south2, wave, amp_west, table, up2, low2,
    )
    moved2 = from_behind(low2, "ty", 1)
    up1, low1 = call(
        west_third_kernel, [pair, pair], info, inner, shifted, phasor, table, up1, low1
    )
    moved1 = from_behind(low1, "ty", 1)
    power = power_up + power_moved
    return jnp.concatenate(
        [
            first + (up1 + moved1) / (power[1:2] + 1.0),
            second + (up2 + moved2) / (power[0:1] + 1.0),
        ]
    )


def solution(mesh):
    return jax.shard_map(
        on_device,
        mesh=mesh,
        in_specs=(
            P(None, ("groups", "ty"), "tx"),
            P(),
            P(),
            P(("groups", "ty"), "tx", None, None),
            P(("groups", "ty"), "tx"),
            P(("groups", "ty"), "tx", None, None, None),
        ),
        out_specs=P(None, ("groups", "ty"), "tx"),
        check_vma=False,
    )
```

time: 133 us -> 91 us (0.68)
  the two profiles are of different devices: /device:TPU:0 before, /device:TPU:12 now
where the time goes in v1:
time: 91 us; the launch traced here: 92.4 us
  starting transfers between devices  38.1 us (42%)
  Pallas kernels  28.3 us (31%)
  waiting for transfers between devices  14.7 us (16%)
  local copies, waits for them, and re-layouts  6.18 us (7%)
  other arithmetic  4.1 us (5%)
  between operations  0.96 us (1%)
    ppermute x15, starting transfers between devices, from_behind(): return lax.ppermute(block, axis, route)  38.1 us
    pallas_call x6, Pallas kernels, call(): pl.pallas_call(kernel, out_shape=[pltpu.VMEM(s, F32) for s in shapes], in...  28.3 us
    ppermute x15, waiting for transfers between devices, from_behind(): return lax.ppermute(block, axis, route)  14.7 us
    unnamed x9, local copies, waits for them, and re-layouts  2.94 us
    add x2, other arithmetic, on_device(): first + (up1 + moved1) / (power[1:2] + 1.0)  2.76 us
    another operation x1, local copies, waits for them, and re-layouts, on_device(): phasor = jnp.stack([jnp.cos(phase), jnp.sin(phase)])  1.86 us
  transfers between devices with their start and end apart: 15, of which 4 were waited for; matrix products, arithmetic and copies ran while one was open for 4% of the time, Pallas kernels for 31%

profile of v1, /device:TPU:12, one launch (start us, length us, event | category | flops | bytes accessed | tf_op | source)
XLA Modules:
  0.0 92.4 jit_solution(18185096206809844870)
XLA Ops:
  0.0 1.3 %fusion.2 = (f32[2,256,256]{2,1,0:T(8,128)S(1)}, f32[2,256,256]{2,1,0:T(8,128)S(1)}) fusion(f32[4,256,256]{2,1,0:T(8,128)} %param.8), kind=kLoop, calls=%fused_computation.12 | loop fusion | bytes 2097152 | tf_op jit(solution)/shard_map/slice | solution.py:302
  1.3 2.4 %collective-permute-start.4 = (f32[2,256,256]{2,1,0:T(8,128)S(1)}, f32[2,256,256]{2,1,0:T(8,128)S(1)}, u32[]{:S(2)}, u32[]{:S(2)}) collective-permute-start(f32[2,256,256]{2,1,0:T(8,128)S(1)} %get-tuple-element.35.own), channel_id=1, source_target_pairs={{1,0},{2,1},{3,2},{5,4},{6,5},{7,6},{9,8},{10,9},{11,10},{13,12},{... | collective-permute-start | bytes 1572872 | tf_op jit(solution)/shard_map/ppermute | solution.py:21
  3.7 3.5 %collective-permute-start.7 = (f32[2,256,256]{2,1,0:T(8,128)S(1)}, f32[2,256,256]{2,1,0:T(8,128)S(1)}, u32[]{:S(2)}, u32[]{:S(2)}) collective-permute-start(f32[2,256,256]{2,1,0:T(8,128)S(1)} %get-tuple-element.35.own), channel_id=1, source_target_pairs={{0,1},{1,2},{2,3},{4,5},{5,6},{6,7},{8,9},{9,10},{10,11},{12,13},{... | collective-permute-start | bytes 1572872 | tf_op jit(solution)/shard_map/ppermute | solution.py:21
  7.2 1.9 %collective-permute-start.5 = (f32[2,256,256]{2,1,0:T(8,128)S(1)}, f32[2,256,256]{2,1,0:T(8,128)S(1)}, u32[]{:S(2)}, u32[]{:S(2)}) collective-permute-start(f32[2,256,256]{2,1,0:T(8,128)S(1)} %get-tuple-element.35.own), channel_id=1, source_target_pairs={{4,0},{8,4},{12,8},{5,1},{9,5},{13,9},{6,2},{10,6},{14,10},{7,3},{... | collective-permute-start | bytes 1572872 | tf_op jit(solution)/shard_map/ppermute | solution.py:21
  9.1 0.8 copy.10
  9.9 0.1 reshape.3
  10.6 0.1 pad_add_fusion.1.info
  10.7 3.5 %collective-permute-start = (s32[1,9]{1,0:T(1,128)S(1)}, s32[1,9]{1,0:T(1,128)S(1)}, u32[]{:S(2)}, u32[]{:S(2)}) collective-permute-start(s32[1,9]{1,0:T(1,128)S(1)} %pad_add_fusion.1.info), channel_id=1, source_target_pairs={{0,1},{1,2},{2,3},{4,5},{5,6},{6,7},{8,9},{9,10},{10,11},{12,13},{... | collective-permute-start | bytes 116 | tf_op jit(solution)/shard_map/ppermute | solution.py:21
  14.2 2.3 %collective-permute-start.10 = (f32[2,256,256]{2,1,0:T(8,128)S(1)}, f32[2,256,256]{2,1,0:T(8,128)S(1)}, u32[]{:S(2)}, u32[]{:S(2)}) collective-permute-start(f32[2,256,256]{2,1,0:T(8,128)S(1)} %get-tuple-element.36.own), channel_id=1, source_target_pairs={{1,0},{2,1},{3,2},{5,4},{6,5},{7,6},{9,8},{10,9},{11,10},{13,12},{... | collective-permute-start | bytes 1572872 | tf_op jit(solution)/shard_map/ppermute | solution.py:21
  16.5 1.9 %cosine_bitcast_fusion = (f32[1,256,256]{2,1,0:T(8,128)S(1)}, f32[1,256,256]{2,1,0:T(8,128)S(1)}) fusion(f32[256,256]{1,0:T(8,128)} %param.10), kind=kLoop, calls=%fused_computation.9 | loop fusion | bytes 786432 | tf_op jit(solution)/shard_map/stack | solution.py:310
  18.4 0.6 collective-permute-done
  19.0 3.5 %collective-permute-start.2 = (f32[2,256,256]{2,1,0:T(8,128)S(1)}, f32[2,256,256]{2,1,0:T(8,128)S(1)}, u32[]{:S(2)}, u32[]{:S(2)}) collective-permute-start(f32[2,256,256]{2,1,0:T(8,128)S(1)} %get-tuple-element.36.own), channel_id=1, source_target_pairs={{0,1},{1,2},{2,3},{4,5},{5,6},{6,7},{8,9},{9,10},{10,11},{12,13},{... | collective-permute-start | bytes 1572872 | tf_op jit(solution)/shard_map/ppermute | solution.py:21
  22.5 0.0 collective-permute-done.4.east
  22.5 1.9 %collective-permute-start.6 = (f32[2,256,256]{2,1,0:T(8,128)S(1)}, f32[2,256,256]{2,1,0:T(8,128)S(1)}, u32[]{:S(2)}, u32[]{:S(2)}) collective-permute-start(f32[2,256,256]{2,1,0:T(8,128)S(1)} %collective-permute-done.4.east), channel_id=1, source_target_pairs={{4,0},{8,4},{12,8},{5,1},{9,5},{13,9},{6,2},{10,6},{14,10},{7,3},{... | collective-permute-start | bytes 1572872 | tf_op jit(solution)/shard_map/ppermute | solution.py:21
  24.4 0.0 collective-permute-done.7.west
  24.4 2.5 %collective-permute-start.8 = (f32[2,256,256]{2,1,0:T(8,128)S(1)}, f32[2,256,256]{2,1,0:T(8,128)S(1)}, u32[]{:S(2)}, u32[]{:S(2)}) collective-permute-start(f32[2,256,256]{2,1,0:T(8,128)S(1)} %collective-permute-done.7.west), channel_id=1, source_target_pairs={{4,0},{8,4},{12,8},{5,1},{9,5},{13,9},{6,2},{10,6},{14,10},{7,3},{... | collective-permute-start | bytes 1572872 | tf_op jit(solution)/shard_map/ppermute | solution.py:21
  27.0 0.0 copy-start
  27.0 1.2 %copy-done = f32[1,1,4,256,256]{4,3,2,1,0:T(8,128)S(1)} copy-done((f32[1,1,4,256,256]{4,3,2,1,0:T(8,128)S(1)}, f32[1,1,4,256,256]{4,3,2,1,0:T(8,128)}, u32[]{:S(2)}) %copy-start) | copy-done | bytes 1048600
  28.2 0.0 copy-start.3
  28.2 0.9 %copy-done.3 = bf16[2,256,256]{2,1,0:T(8,128)(2,1)S(1)} copy-done((bf16[2,256,256]{2,1,0:T(8,128)(2,1)S(1)}, bf16[2,256,256]{2,1,0:T(8,128)(2,1)}, u32[]{:S(2)}) %copy-start.3) | copy-done | bytes 262168
  29.1 0.0 copy-start.1
  29.1 1.7 %shard_map.83 = (f32[4,256,256]{2,1,0:T(8,128)S(1)}, f32[2,256,256]{2,1,0:T(8,128)S(1)}) custom-call(s32[1,9]{1,0:T(1,128)S(1)} %pad_add_fusion.1.info, f32[4,256,256]{2,1,0:T(8,128)S(1)} %bitcast.9, f32[2,256,256]{2,1,0:T(8,128)S(1)} %pad_maximum_fusion.1.phasor, bf16[2,256,256]{2,1,0:T(8,128)(2,1)S(1)} %copy-done.3), custom_call_target="tpu_custom_call" | custom-call | flops 4000000000 | bytes 4000000 | tf_op jit(solution)/shard_map/pallas_call | solution.py:280
  30.9 0.1 pad_add_fusion.info
  31.0 0.0 copy-done.1
  31.0 0.0 copy-start.2
  31.0 1.7 %shard_map.82.shifted = f32[2,4,2,256,256]{4,3,2,1,0:T(8,128)S(1)} custom-call(s32[2,9]{1,0:T(2,128)S(1)} %pad_add_fusion.info, f32[2,256,256]{2,1,0:T(8,128)S(1)} %copy-done.1), custom_call_target="tpu_custom_call" | custom-call | flops 4000000000 | bytes 4000000 | tf_op jit(solution)/shard_map/pallas_call | solution.py:280
  32.7 0.0 collective-permute-done.5.south
  32.7 2.2 %collective-permute-start.1 = (f32[2,256,256]{2,1,0:T(8,128)S(1)}, f32[2,256,256]{2,1,0:T(8,128)S(1)}, u32[]{:S(2)}, u32[]{:S(2)}) collective-permute-start(f32[2,256,256]{2,1,0:T(8,128)S(1)} %get-tuple-element.36.own), channel_id=1, source_target_pairs={{4,0},{8,4},{12,8},{5,1},{9,5},{13,9},{6,2},{10,6},{14,10},{7,3},{... | collective-permute-start | bytes 1572872 | tf_op jit(solution)/shard_map/ppermute | solution.py:21
  35.0 0.0 collective-permute-done.10.east
  35.0 4.8 %collective-permute-start.9 = (f32[4,256,256]{2,1,0:T(8,128)S(1)}, f32[4,256,256]{2,1,0:T(8,128)S(1)}, u32[]{:S(2)}, u32[]{:S(2)}) collective-permute-start(f32[4,256,256]{2,1,0:T(8,128)S(1)} %get-tuple-element.21.amp), channel_id=1, source_target_pairs={{0,1},{1,2},{2,3},{4,5},{5,6},{6,7},{8,9},{9,10},{10,11},{12,13},{... | collective-permute-start | bytes 3145736 | tf_op jit(solution)/shard_map/ppermute | solution.py:21
  39.8 0.0 collective-permute-done.2.west
  39.8 1.9 %collective-permute-start.11 = (f32[2,256,256]{2,1,0:T(8,128)S(1)}, f32[2,256,256]{2,1,0:T(8,128)S(1)}, u32[]{:S(2)}, u32[]{:S(2)}) collective-permute-start(f32[2,256,256]{2,1,0:T(8,128)S(1)} %collective-permute-done.10.east), channel_id=1, source_target_pairs={{4,0},{8,4},{12,8},{5,1},{9,5},{13,9},{6,2},{10,6},{14,10},{7,3},{... | collective-permute-start | bytes 1572872 | tf_op jit(solution)/shard_map/ppermute | solution.py:21
  41.8 0.0 collective-permute-done.6.corner
  41.8 1.9 %collective-permute-start.3 = (f32[2,256,256]{2,1,0:T(8,128)S(1)}, f32[2,256,256]{2,1,0:T(8,128)S(1)}, u32[]{:S(2)}, u32[]{:S(2)}) collective-permute-start(f32[2,256,256]{2,1,0:T(8,128)S(1)} %collective-permute-done.2.west), channel_id=1, source_target_pairs={{4,0},{8,4},{12,8},{5,1},{9,5},{13,9},{6,2},{10,6},{14,10},{7,3},{... | collective-permute-start | bytes 1572872 | tf_op jit(solution)/shard_map/ppermute | solution.py:21
  43.7 0.0 collective-permute-done.8.west_south
  43.7 0.0 copy-done.2
  43.7 8.8 %shard_map.84 = (f32[2,4,2,256,256]{4,3,2,1,0:T(8,128)S(1)}, f32[2,256,256]{2,1,0:T(8,128)S(1)}, f32[2,256,256]{2,1,0:T(8,128)}) custom-call(s32[2,9]{1,0:T(2,128)S(1)} %pad_add_fusion.info, f32[2,256,256]{2,1,0:T(8,128)S(1)} %get-tuple-element.35.own, f32[2,256,256]{2,1,0:T(8,128)S(1)} %collective-permute-done.4.east, ...), custom_call_target="tpu_custom_call" | custom-call | flops 10000000000 | bytes 10000000 | tf_op jit(solution)/shard_map/pallas_call | solution.py:280
  52.5 1.9 %collective-permute-start.13 = (f32[2,256,256]{2,1,0:T(8,128)}, f32[2,256,256]{2,1,0:T(8,128)}, u32[]{:S(2)}, u32[]{:S(2)}) collective-permute-start(f32[2,256,256]{2,1,0:T(8,128)} %get-tuple-element.30), channel_id=1, source_target_pairs={{0,4},{4,8},{8,12},{1,5},{5,9},{9,13},{2,6},{6,10},{10,14},{3,7},{... | collective-permute-start | bytes 1572872 | tf_op jit(solution)/shard_map/ppermute | solution.py:21
  54.5 0.0 collective-permute-done.1.south
  54.5 0.0 collective-permute-done.11.corner
  54.5 5.5 %shard_map.85 = (f32[2,256,256]{2,1,0:T(8,128)S(1)}, f32[2,256,256]{2,1,0:T(8,128)S(1)}, f32[2,256,256]{2,1,0:T(8,128)S(1)}, f32[2,256,256]{2,1,0:T(8,128)S(1)}) custom-call(s32[2,9]{1,0:T(2,128)S(1)} %pad_add_fusion.info, f32[2,256,256]{2,1,0:T(8,128)S(1)} %get-tuple-element.36.own, f32[2,256,256]{2,1,0:T(8,128)S(1)} %collective-permute-done.10.east, ...), custom_call_target="tpu_custom_call" | custom-call | flops 10000000000 | bytes 10000000 | tf_op jit(solution)/shard_map/pallas_call | solution.py:280
  60.0 2.9 %collective-permute-done.9.amp = f32[4,256,256]{2,1,0:T(8,128)S(1)} collective-permute-done((f32[4,256,256]{2,1,0:T(8,128)S(1)}, f32[4,256,256]{2,1,0:T(8,128)S(1)}, u32[]{:S(2)}, u32[]{:S(2)}) %collective-permute-start.9) | collective-permute-done | bytes 1048608 | tf_op jit(solution)/shard_map/ppermute | solution.py:21
  62.9 0.0 collective-permute-done.3.west_south
  62.9 5.7 %shard_map.86 = (f32[4,2,256,256]{3,2,1,0:T(8,128)S(1)}, f32[2,256,256]{2,1,0:T(8,128)S(1)}, f32[2,256,256]{2,1,0:T(8,128)S(1)}) custom-call(s32[2,9]{1,0:T(2,128)S(1)} %pad_add_fusion.info, f32[2,256,256]{2,1,0:T(8,128)S(1)} %get-tuple-element.36.own, f32[2,256,256]{2,1,0:T(8,128)S(1)} %collective-permute-done.1.south, ...), custom_call_target="tpu_custom_call" | custom-call | flops 4000000000 | bytes 4000000 | tf_op jit(solution)/shard_map/pallas_call | solution.py:280
  68.6 4.8 %shard_map.87 = (f32[2,256,256]{2,1,0:T(8,128)S(1)}, f32[2,256,256]{2,1,0:T(8,128)S(1)}) custom-call(s32[2,9]{1,0:T(2,128)S(1)} %pad_add_fusion.info, f32[4,2,256,256]{3,2,1,0:T(8,128)S(1)} %get-tuple-element.24.inner, f32[2,4,2,256,256]{4,3,2,1,0:T(8,128)S(1)} %shard_map.82.shifted, f32[2,256,256]{2,1,0:T(8,128)S(1)} %get-tuple-element.19.phasor, ...), custom_call_target="tpu_custom_call" | custom-call | flops 4000000000 | bytes 4000000 | tf_op jit(solution)/shard_map/pallas_call | solution.py:280
  73.4 1.9 %collective-permute-start.12 = (f32[2,256,256]{2,1,0:T(8,128)S(1)}, f32[2,256,256]{2,1,0:T(8,128)}, u32[]{:S(2)}, u32[]{:S(2)}) collective-permute-start(f32[2,256,256]{2,1,0:T(8,128)S(1)} %get-tuple-element.28), channel_id=1, source_target_pairs={{0,4},{4,8},{8,12},{1,5},{5,9},{9,13},{2,6},{6,10},{10,14},{3,7},{... | collective-permute-start | bytes 1572872 | tf_op jit(solution)/shard_map/ppermute | solution.py:21
  75.3 1.9 %collective-permute-start.14 = (f32[2,256,256]{2,1,0:T(8,128)S(1)}, f32[2,256,256]{2,1,0:T(8,128)}, u32[]{:S(2)}, u32[]{:S(2)}) collective-permute-start(f32[2,256,256]{2,1,0:T(8,128)S(1)} %get-tuple-element.32), channel_id=1, source_target_pairs={{0,4},{4,8},{8,12},{1,5},{5,9},{9,13},{2,6},{6,10},{10,14},{3,7},{... | collective-permute-start | bytes 1572872 | tf_op jit(solution)/shard_map/ppermute | solution.py:21
  77.3 0.0 collective-permute-done.13
  77.3 1.1 %add.22 = f32[2,256,256]{2,1,0:T(8,128)S(1)} add(f32[2,256,256]{2,1,0:T(8,128)S(1)} %get-tuple-element.29, f32[2,256,256]{2,1,0:T(8,128)} %collective-permute-done.13) | non-fusion elementwise | flops 131072 | bytes 1572864 | tf_op jit(solution)/shard_map/add | solution.py:343
  78.5 5.6 %collective-permute-done.12 = f32[2,256,256]{2,1,0:T(8,128)} collective-permute-done((f32[2,256,256]{2,1,0:T(8,128)S(1)}, f32[2,256,256]{2,1,0:T(8,128)}, u32[]{:S(2)}, u32[]{:S(2)}) %collective-permute-start.12) | collective-permute-done | bytes 524320 | tf_op jit(solution)/shard_map/ppermute | solution.py:21
  84.0 5.6 %collective-permute-done.14 = f32[2,256,256]{2,1,0:T(8,128)} collective-permute-done((f32[2,256,256]{2,1,0:T(8,128)S(1)}, f32[2,256,256]{2,1,0:T(8,128)}, u32[]{:S(2)}, u32[]{:S(2)}) %collective-permute-start.14) | collective-permute-done | bytes 524320 | tf_op jit(solution)/shard_map/ppermute | solution.py:21
  89.6 2.8 %divide_add_fusion.1 = (f32[4,256,256]{2,1,0:T(8,128)}, f32[4,256,256]{2,1,0:T(8,128)}) fusion(f32[2,256,256]{2,1,0:T(8,128)S(1)} %get-tuple-element.27, f32[2,256,256]{2,1,0:T(8,128)} %collective-permute-done.12, f32[256,256]{1,0:T(8,128)S(1)} %get-tuple-element.37, f32[4,256,256]{2,1,0:T(8,128)} %param.8, ...), kind=kLoop, output_to_operand_aliasing={{0}: (7, {}), {1}: (7, {})}, calls=%fused_computation.3 | loop fusion | flops 786432 | bytes 4718592 | tf_op jit(solution)/shard_map/add | solution.py:346
  (3 shorter events, 0.1 us)
Async XLA Ops:
  1.3 21.2 %collective-permute-start.4 = (f32[2,256,256]{2,1,0:T(8,128)S(1)}, f32[2,256,256]{2,1,0:T(8,128)S(1)}, u32[]{:S(2)}, u32[]{:S(2)}) collective-permute-start(f32[2,256,256]{2,1,0:T(8,128)S(1)} %get-tuple-element.35.own), channel_id=1, source_target_pairs={{1,0},{2,1},{3,2},{5,4},{6,5},{7,6},{9,8},{10,9},{11,10},{13,12},{... | collective-permute-start | bytes 1572872 | tf_op jit(solution)/shard_map/ppermute | solution.py:21
  3.7 20.8 %collective-permute-start.7 = (f32[2,256,256]{2,1,0:T(8,128)S(1)}, f32[2,256,256]{2,1,0:T(8,128)S(1)}, u32[]{:S(2)}, u32[]{:S(2)}) collective-permute-start(f32[2,256,256]{2,1,0:T(8,128)S(1)} %get-tuple-element.35.own), channel_id=1, source_target_pairs={{0,1},{1,2},{2,3},{4,5},{5,6},{6,7},{8,9},{9,10},{10,11},{12,13},{... | collective-permute-start | bytes 1572872 | tf_op jit(solution)/shard_map/ppermute | solution.py:21
  7.2 25.6 %collective-permute-start.5 = (f32[2,256,256]{2,1,0:T(8,128)S(1)}, f32[2,256,256]{2,1,0:T(8,128)S(1)}, u32[]{:S(2)}, u32[]{:S(2)}) collective-permute-start(f32[2,256,256]{2,1,0:T(8,128)S(1)} %get-tuple-element.35.own), channel_id=1, source_target_pairs={{4,0},{8,4},{12,8},{5,1},{9,5},{13,9},{6,2},{10,6},{14,10},{7,3},{... | collective-permute-start | bytes 1572872 | tf_op jit(solution)/shard_map/ppermute | solution.py:21
  10.7 8.3 %collective-permute-start = (s32[1,9]{1,0:T(1,128)S(1)}, s32[1,9]{1,0:T(1,128)S(1)}, u32[]{:S(2)}, u32[]{:S(2)}) collective-permute-start(s32[1,9]{1,0:T(1,128)S(1)} %pad_add_fusion.1.info), channel_id=1, source_target_pairs={{0,1},{1,2},{2,3},{4,5},{5,6},{6,7},{8,9},{9,10},{10,11},{12,13},{... | collective-permute-start | bytes 116 | tf_op jit(solution)/shard_map/ppermute | solution.py:21
  14.2 20.8 %collective-permute-start.10 = (f32[2,256,256]{2,1,0:T(8,128)S(1)}, f32[2,256,256]{2,1,0:T(8,128)S(1)}, u32[]{:S(2)}, u32[]{:S(2)}) collective-permute-start(f32[2,256,256]{2,1,0:T(8,128)S(1)} %get-tuple-element.36.own), channel_id=1, source_target_pairs={{1,0},{2,1},{3,2},{5,4},{6,5},{7,6},{9,8},{10,9},{11,10},{13,12},{... | collective-permute-start | bytes 1572872 | tf_op jit(solution)/shard_map/ppermute | solution.py:21
  19.0 20.8 %collective-permute-start.2 = (f32[2,256,256]{2,1,0:T(8,128)S(1)}, f32[2,256,256]{2,1,0:T(8,128)S(1)}, u32[]{:S(2)}, u32[]{:S(2)}) collective-permute-start(f32[2,256,256]{2,1,0:T(8,128)S(1)} %get-tuple-element.36.own), channel_id=1, source_target_pairs={{0,1},{1,2},{2,3},{4,5},{5,6},{6,7},{8,9},{9,10},{10,11},{12,13},{... | collective-permute-start | bytes 1572872 | tf_op jit(solution)/shard_map/ppermute | solution.py:21
  22.5 19.3 %collective-permute-start.6 = (f32[2,256,256]{2,1,0:T(8,128)S(1)}, f32[2,256,256]{2,1,0:T(8,128)S(1)}, u32[]{:S(2)}, u32[]{:S(2)}) collective-permute-start(f32[2,256,256]{2,1,0:T(8,128)S(1)} %collective-permute-done.4.east), channel_id=1, source_target_pairs={{4,0},{8,4},{12,8},{5,1},{9,5},{13,9},{6,2},{10,6},{14,10},{7,3},{... | collective-permute-start | bytes 1572872 | tf_op jit(solution)/shard_map/ppermute | solution.py:21
  24.4 19.3 %collective-permute-start.8 = (f32[2,256,256]{2,1,0:T(8,128)S(1)}, f32[2,256,256]{2,1,0:T(8,128)S(1)}, u32[]{:S(2)}, u32[]{:S(2)}) collective-permute-start(f32[2,256,256]{2,1,0:T(8,128)S(1)} %collective-permute-done.7.west), channel_id=1, source_target_pairs={{4,0},{8,4},{12,8},{5,1},{9,5},{13,9},{6,2},{10,6},{14,10},{7,3},{... | collective-permute-start | bytes 1572872 | tf_op jit(solution)/shard_map/ppermute | solution.py:21
  27.0 1.2 %copy-start = (f32[1,1,4,256,256]{4,3,2,1,0:T(8,128)S(1)}, f32[1,1,4,256,256]{4,3,2,1,0:T(8,128)}, u32[]{:S(2)}) copy-start(f32[1,1,4,256,256]{4,3,2,1,0:T(8,128)} %param.13) | copy-start | bytes 3145732
  28.2 0.9 %copy-start.3 = (bf16[2,256,256]{2,1,0:T(8,128)(2,1)S(1)}, bf16[2,256,256]{2,1,0:T(8,128)(2,1)}, u32[]{:S(2)}) copy-start(bf16[2,256,256]{2,1,0:T(8,128)(2,1)} %constant.7.clone.order) | copy-start | bytes 786436
  29.1 1.8 %copy-start.1 = (f32[2,256,256]{2,1,0:T(8,128)S(1)}, f32[2,256,256]{2,1,0:T(8,128)}, u32[]{:S(2)}) copy-start(f32[2,256,256]{2,1,0:T(8,128)} %probe.1) | copy-start | bytes 1572868
  31.0 12.7 %copy-start.2 = (bf16[8,256,256]{2,1,0:T(8,128)(2,1)S(1)}, bf16[8,256,256]{2,1,0:T(8,128)(2,1)}, u32[]{:S(2)}) copy-start(bf16[8,256,256]{2,1,0:T(8,128)(2,1)} %constant.6.clone.table) | copy-start | bytes 3145732
  32.7 21.7 %collective-permute-start.1 = (f32[2,256,256]{2,1,0:T(8,128)S(1)}, f32[2,256,256]{2,1,0:T(8,128)S(1)}, u32[]{:S(2)}, u32[]{:S(2)}) collective-permute-start(f32[2,256,256]{2,1,0:T(8,128)S(1)} %get-tuple-element.36.own), channel_id=1, source_target_pairs={{4,0},{8,4},{12,8},{5,1},{9,5},{13,9},{6,2},{10,6},{14,10},{7,3},{... | collective-permute-start | bytes 1572872 | tf_op jit(solution)/shard_map/ppermute | solution.py:21
  35.0 27.9 %collective-permute-start.9 = (f32[4,256,256]{2,1,0:T(8,128)S(1)}, f32[4,256,256]{2,1,0:T(8,128)S(1)}, u32[]{:S(2)}, u32[]{:S(2)}) collective-permute-start(f32[4,256,256]{2,1,0:T(8,128)S(1)} %get-tuple-element.21.amp), channel_id=1, source_target_pairs={{0,1},{1,2},{2,3},{4,5},{5,6},{6,7},{8,9},{9,10},{10,11},{12,13},{... | collective-permute-start | bytes 3145736 | tf_op jit(solution)/shard_map/ppermute | solution.py:21
  39.8 14.6 %collective-permute-start.11 = (f32[2,256,256]{2,1,0:T(8,128)S(1)}, f32[2,256,256]{2,1,0:T(8,128)S(1)}, u32[]{:S(2)}, u32[]{:S(2)}) collective-permute-start(f32[2,256,256]{2,1,0:T(8,128)S(1)} %collective-permute-done.10.east), channel_id=1, source_target_pairs={{4,0},{8,4},{12,8},{5,1},{9,5},{13,9},{6,2},{10,6},{14,10},{7,3},{... | collective-permute-start | bytes 1572872 | tf_op jit(solution)/shard_map/ppermute | solution.py:21
  41.8 21.1 %collective-permute-start.3 = (f32[2,256,256]{2,1,0:T(8,128)S(1)}, f32[2,256,256]{2,1,0:T(8,128)S(1)}, u32[]{:S(2)}, u32[]{:S(2)}) collective-permute-start(f32[2,256,256]{2,1,0:T(8,128)S(1)} %collective-permute-done.2.west), channel_id=1, source_target_pairs={{4,0},{8,4},{12,8},{5,1},{9,5},{13,9},{6,2},{10,6},{14,10},{7,3},{... | collective-permute-start | bytes 1572872 | tf_op jit(solution)/shard_map/ppermute | solution.py:21
  52.5 24.8 %collective-permute-start.13 = (f32[2,256,256]{2,1,0:T(8,128)}, f32[2,256,256]{2,1,0:T(8,128)}, u32[]{:S(2)}, u32[]{:S(2)}) collective-permute-start(f32[2,256,256]{2,1,0:T(8,128)} %get-tuple-element.30), channel_id=1, source_target_pairs={{0,4},{4,8},{8,12},{1,5},{5,9},{9,13},{2,6},{6,10},{10,14},{3,7},{... | collective-permute-start | bytes 1572872 | tf_op jit(solution)/shard_map/ppermute | solution.py:21
  73.4 10.6 %collective-permute-start.12 = (f32[2,256,256]{2,1,0:T(8,128)S(1)}, f32[2,256,256]{2,1,0:T(8,128)}, u32[]{:S(2)}, u32[]{:S(2)}) collective-permute-start(f32[2,256,256]{2,1,0:T(8,128)S(1)} %get-tuple-element.28), channel_id=1, source_target_pairs={{0,4},{4,8},{8,12},{1,5},{5,9},{9,13},{2,6},{6,10},{10,14},{3,7},{... | collective-permute-start | bytes 1572872 | tf_op jit(solution)/shard_map/ppermute | solution.py:21
  75.3 14.3 %collective-permute-start.14 = (f32[2,256,256]{2,1,0:T(8,128)S(1)}, f32[2,256,256]{2,1,0:T(8,128)}, u32[]{:S(2)}, u32[]{:S(2)}) collective-permute-start(f32[2,256,256]{2,1,0:T(8,128)S(1)} %get-tuple-element.32), channel_id=1, source_target_pairs={{0,4},{4,8},{8,12},{1,5},{5,9},{9,13},{2,6},{6,10},{10,14},{3,7},{... | collective-permute-start | bytes 1572872 | tf_op jit(solution)/shard_map/ppermute | solution.py:21
